TPU v7x, 256 devices: a whole 4x4x8 slice. The times are simulated.
256 devices in a mesh: var: 4 (over y), tok: 64 (over x, z, core).
Axes of the slice: x: 4, y: 4, z: 8, core: 2. Of those that a mesh axis runs over, the one named last changes fastest.
Arguments:
- tokens: bfloat16 [8, 16384, 8192], P('var', 'tok'), may hold values from -16 to 16
- up_panel: bfloat16 [8, 8192, 1024], P('var', 'tok'), may hold values from -6 to 6
Outputs:
- gram_sum: float32 [256, 8192], P('var', 'tok')
- numerator: float32 [256, 1024], P(('var', 'tok'))
All inputs are finite; a program needn't handle non-finite values.
Results may differ from a plain program's by a relative error of at most 0.00045.
Values may be sent and summed in bfloat16 or wider, within the bound.
A program may use at most 128 MiB of HBM per device.

v0:
```python
import jax
import jax.numpy as jnp
from jax import lax
from jax.sharding import PartitionSpec as P

WINDOW = 256


def body(tokens, up_panel):
    var_count, tok_count, width = tokens.shape
    groups = lax.axis_size("tok")
    block = width // groups
    total = tok_count * groups
    scale = 1.0 / total
    window = tokens[:, :, :WINDOW]
    product = jnp.einsum("vtc,vtg->cvg", tokens, window, preferred_element_type=jnp.float32)
    summed = lax.psum_scatter(
        product.reshape(block * lax.axis_size("tok"), var_count * WINDOW),
        "tok",
        scatter_dimension=0,
        tiled=True,
    )
    blocks = summed.reshape(block, var_count, WINDOW).transpose(1, 2, 0)
    blocks = blocks * scale
    gram_sum = lax.psum_scatter(jnp.sum(blocks, axis=0), "var", scatter_dimension=0, tiled=True)
    terms = jnp.einsum(
        "vgc,vcp->gp", blocks, up_panel.astype(jnp.float32), precision=lax.Precision.HIGHEST
    )
    numerator = lax.psum_scatter(terms, ("var", "tok"), scatter_dimension=0, tiled=True)
    return (gram_sum, numerator)


def solution(mesh):
    return jax.shard_map(
        body,
        mesh=mesh,
        in_specs=(P("var", "tok", None), P("var", "tok", None)),
        out_specs=(P("var", "tok"), P(("var", "tok"), None)),
        check_vma=False,
    )
```

profile of v0, /device:TPU:1, one launch (start us, length us, event | category | flops | bytes accessed | tf_op | source)
XLA Modules:
  0.0 501.1 jit_solution(12597069937436537269)
XLA Ops:
  7.2 0.0 copy-start
  7.2 0.0 reduce-scatter.3.cloned.1.call-start
  7.2 11.6 %fusion = f32[2,256,8192]{2,1,0:T(8,128)} fusion(bf16[2,256,8192]{2,1,0:T(8,128)(2,1)} %param.2), kind=kOutput, calls=%fused_computation.1 | convolution fusion | flops 2147483648 | bytes 25427968 | tf_op jit(solution)/shard_map/vtc,vtg->cvg/dot_general | solution.py:16
  18.8 0.0 reduce-scatter.3.cloned.1.call-update
  18.9 0.0 all-reduce.3.cloned.1.call-start
  18.9 189.2 %reduce-scatter.3.cloned.1.call-done = f32[128,512]{0,1:T(8,128)} async-done(((f32[8192,512]{0,1:T(8,128)}), f32[128,512]{0,1:T(8,128)}) %reduce-scatter.3.cloned.1.call-update) | async-done | bytes 262160 | tf_op jit(solution)/shard_map/reduce_scatter | solution.py:17
  208.1 1.0 broadcast_multiply_fusion
  209.1 0.0 copy-done
  209.1 1.6 convolution_bitcast_fusion
  210.8 0.0 all-reduce.3.cloned.1.call-update
  210.8 0.0 reduce-scatter.5.cloned.1.call-start
  210.8 0.7 reduce_sum.9
  211.5 0.0 reduce-scatter.5.cloned.1.call-update
  211.5 258.9 %all-reduce.3.cloned.1.call-done = f32[256,1024]{1,0:T(8,128)} async-done(((f32[256,1024]{1,0:T(8,128)}), f32[256,1024]{1,0:T(8,128)}) %all-reduce.3.cloned.1.call-update) | async-done | bytes 1048592
  470.4 1.4 constant_dynamic-slice_fusion
  471.7 22.8 %reduce-scatter.5.cloned.1.call-done = f32[64,128]{1,0:T(8,128)} async-done(((f32[256,128]{1,0:T(8,128)}), f32[64,128]{1,0:T(8,128)}) %reduce-scatter.5.cloned.1.call-update) | async-done | bytes 32784 | tf_op jit(solution)/shard_map/reduce_scatter | solution.py:25
Async XLA Ops:
  7.2 202.0 %copy-start = (bf16[2,128,1024]{2,1,0:T(8,128)(2,1)S(1)}, bf16[2,128,1024]{2,1,0:T(8,128)(2,1)}, u32[]{:S(2)}) copy-start(bf16[2,128,1024]{2,1,0:T(8,128)(2,1)} %param.3) | copy-start | bytes 1572868
  7.2 201.0 %reduce-scatter.3.cloned.1.call-start = ((), (), s32[]{:S(2)}) async-start(), calls=%async_computation.2 | async-start | bytes 17039360 | tf_op jit(solution)/shard_map/reduce_scatter | solution.py:17
  18.9 451.5 %all-reduce.3.cloned.1.call-start = ((), (), s32[]{:S(2)}) async-start(), calls=%async_computation.4 | async-start | bytes 2097152
  210.8 283.8 %reduce-scatter.5.cloned.1.call-start = ((), (), s32[]{:S(2)}) async-start(), calls=%async_computation.3 | async-start | bytes 163840 | tf_op jit(solution)/shard_map/reduce_scatter | solution.py:25
Sparse Core Ops, SparseCore 0:
  19.0 189.1 reduce-scatter.2
  213.6 256.7 all-reduce.2
  473.6 20.9 reduce-scatter.4
where the time goes:
time: 503 us; the launch traced here: 501 us
  waiting for transfers between devices  471 us (94%)
  between operations  13.8 us (3%)
  matrix products  13.2 us (3%)
    unnamed x4, waiting for transfers between devices  259 us
    reduce_scatter x1, waiting for transfers between devices, body(): lax.psum_scatter(product.reshape(block * lax.axis_size('tok'), var_count...  189 us
    reduce_scatter x1, waiting for transfers between devices, body(): lax.psum_scatter(jnp.sum(blocks, axis=0), 'var', scatter_dimension=0, til...  22.8 us
    dot_general x1, matrix products, body(): jnp.einsum('vtc,vtg->cvg', tokens, window, preferred_element_type=jnp.flo...  11.6 us
  transfers between devices with their start and end apart: 3, of which 3 were waited for; matrix products, arithmetic and copies ran while one was open for 0% of the time, Pallas kernels for 0%

commit v1 on v0

v1 whole, which is shorter than its diff:
```python
import functools

import jax
import jax.numpy as jnp
from jax import lax
from jax.experimental import pallas as pl
from jax.experimental.pallas import tpu as pltpu
from jax.sharding import PartitionSpec as P

WINDOW = 256
NX, NZ, NY = 4, 8, 4
CHIPS = NX * NZ
UNIT = 16
UNITS = WINDOW // UNIT
KA = 7
KB = UNITS - KA
K = max(KA, KB)
PIECES = 8
POWER = 9
TOP = 2.0**13.8
MESH = pl.DeviceIdType.MESH
F32, BF16 = jnp.float32, jnp.bfloat16


def encode(value, factor):
    t = value * factor
    t2 = t * t
    t4 = t2 * t2
    return (t4 * t4 * t).astype(BF16)


def decode(code, factor):
    y = code.astype(F32)
    root = jnp.exp2(jnp.log(jnp.maximum(jnp.abs(y), 1e-38)) * (1.4426950408889634 / POWER))
    return jnp.where(y < 0, -root, root) * factor


class Ring:
    def __init__(self, n, blocks, units, me, device, base, source, refs):
        self.n, self.half, self.blocks, self.units = n, n // 2, blocks, units
        self.me, self.device, self.base, self.source = me, device, base, source
        (self.s0, self.sn, self.r0, self.rn, self.bs, self.br, self.enc, self.dec,
         self.send_sem, self.recv_sem, self.bsend_sem, self.brecv_sem) = refs

    @staticmethod
    def scratch(n, blocks, units):
        half = n // 2
        first = pltpu.VMEM((units, 2, blocks, UNIT, 128), BF16)
        later = pltpu.VMEM((units, 2, half - 1, 2, blocks, UNIT, 128), BF16)
        bound = pltpu.VMEM((2, half, UNIT, 128), F32)
        return [first, later, first, later, bound, bound, bound, bound,
                pltpu.SemaphoreType.DMA((2,)), pltpu.SemaphoreType.DMA((units, 2, half)),
                pltpu.SemaphoreType.DMA, pltpu.SemaphoreType.DMA((2, half))]

    def data_copy(self, k, d, s, to):
        if s == 0:
            src, dst = self.s0.at[k, d], self.r0.at[k, d]
        else:
            src, dst = self.sn.at[k, d, s - 1], self.rn.at[k, d, s - 1]
        return pltpu.make_async_remote_copy(
            src_ref=src, dst_ref=dst, send_sem=self.send_sem.at[min(s, 1)],
            recv_sem=self.recv_sem.at[k, d, s], device_id=to, device_id_type=MESH)

    def bound_copy(self, d, s, to):
        return pltpu.make_async_remote_copy(
            src_ref=self.bs.at[d, s], dst_ref=self.br.at[d, s], send_sem=self.bsend_sem,
            recv_sem=self.brecv_sem.at[d, s], device_id=to, device_id_type=MESH)

    def neighbour(self, d):
        return self.device(lax.rem(self.me + (1 if d == 0 else self.n - 1), self.n))

    def arrived(self, k, d, s):
        self.data_copy(k, d, s, self.neighbour(d)).wait_recv()

    def send(self, s, k):
        for d in (0, 1):
            to = self.neighbour(d)
            far = self.half - s
            dest = lax.rem(self.me + (far if d == 0 else self.n - far), self.n)
            if s > 0:
                self.arrived(k, d, s - 1)

            @pl.when(k == 0)
            def _():
                bound = self.base[...]
                if s > 0:
                    self.bound_copy(d, s - 1, to).wait_recv()
                    came = self.br[d, s - 1]
                    self.dec[d, s - 1] = came * (1.0 / TOP)
                    bound = bound + came
                self.bs[d, s] = bound
                self.enc[d, s] = TOP / bound
                self.bound_copy(d, s, to).start()

            enc = self.enc[d, s]
            if s == 0:
                self.s0[k, d] = encode(self.source(dest, d, k), enc)
            else:
                dec = self.dec[d, s - 1]
                for h in (0, 1):
                    value = self.source(dest, h, k)
                    if s > 1:
                        value = value + decode(self.rn[k, d, s - 2, h], dec)
                    elif h == d:
                        value = value + decode(self.r0[k, d], dec)
                    self.sn[k, d, s - 1, h] = encode(value, enc)
            self.data_copy(k, d, s, to).start()

    def finish(self, k, total, store):
        last = self.half - 1
        for d in (0, 1):
            self.arrived(k, d, last)

        @pl.when(k == 0)
        def _():
            for d in (0, 1):
                self.bound_copy(d, last, self.neighbour(d)).wait_recv()
                self.dec[d, last] = self.br[d, last] * (1.0 / TOP)
            if total is not None:
                total[...] = self.base[...] + self.br[0, last] + self.br[1, last]

        for h in (0, 1):
            value = self.source(self.me, h, k)
            for d in (0, 1):
                value = value + decode(self.rn[k, d, last - 1, h], self.dec[d, last])
            store(h, value)

    def sent(self):
        to = self.neighbour(0)
        for src, dst, sem in ((self.s0, self.r0, self.send_sem.at[0]), (self.sn, self.rn, self.send_sem.at[1]),
                              (self.bs, self.br, self.bsend_sem)):
            pltpu.make_async_remote_copy(src_ref=src, dst_ref=dst, send_sem=sem, recv_sem=sem,
                                         device_id=to, device_id_type=MESH).wait_send()


SHAPES = ((NZ, NX, KA), (NX, 1, KA), (NX, NZ, KB), (NZ, 1, KB))


def kernel(scale, tokens, up, gram, num, own, other, wt, upv, prod, base, base_a, base_b, mid_a, mid_b, fin,
           msg1, recv1, msg2, recv2, gacc, own_sem, other_send, other_recv, up_sem, up_send, up_recv,
           send1, sem1, send2, sem2, *ring_refs):
    y, t = lax.axis_index("var"), lax.axis_index("tok")
    c = lax.rem(t, 2)
    chip = t // 2
    z, x = lax.rem(chip, NZ), chip // NZ
    oc = 1 - c
    sibling = (y, chip * 2 + oc)
    width = own.shape[1]
    part = width // PIECES
    depth = own.shape[0]

    def own_copy(i):
        cols = pl.ds(pl.multiple_of(i * part, part), part)
        return pltpu.make_async_copy(tokens.at[c, :, cols], own.at[:, cols], own_sem.at[i])

    def other_copy(i):
        cols = pl.ds(pl.multiple_of(i * part, part), part)
        return pltpu.make_async_remote_copy(
            src_ref=tokens.at[oc, :, cols], dst_ref=other.at[:, cols], send_sem=other_send,
            recv_sem=other_recv.at[i], device_id=sibling, device_id_type=MESH)

    up_own = pltpu.make_async_copy(up.at[c], upv.at[c], up_sem)
    up_other = pltpu.make_async_remote_copy(src_ref=up.at[oc], dst_ref=upv.at[c], send_sem=up_send,
                                            recv_sem=up_recv, device_id=sibling, device_id_type=MESH)
    for i in range(PIECES):
        own_copy(i).start()
    up_own.start()

    barrier = pltpu.get_barrier_semaphore()

    def greet_chip(o, carry):
        pl.semaphore_signal(barrier, inc=1, device_id=(y, lax.rem(chip + o, CHIPS) * 2 + c), device_id_type=MESH)
        return carry

    def pair_of(o):
        pc = lax.rem(y * 2 + c + o, 2 * NY)
        return pc, (pc // 2, chip * 2 + lax.rem(pc, 2))

    def greet_pair(o, carry):
        pl.semaphore_signal(barrier, inc=1, device_id=pair_of(o)[1], device_id_type=MESH)
        return carry

    lax.fori_loop(1, CHIPS, greet_chip, 0)
    lax.fori_loop(1, 2 * NY, greet_pair, 0)
    pl.semaphore_wait(barrier, CHIPS - 1 + 2 * NY - 1)

    for i in range(PIECES):
        other_copy(i).start()
    up_other.start()

    row = lax.broadcasted_iota(jnp.int32, (WINDOW, WINDOW), 0)
    col = lax.broadcasted_iota(jnp.int32, (WINDOW, WINDOW), 1)
    feature = ((row >> 2) & 3) * (WINDOW // NY) + (row >> 4) * 4 + (row & 3)
    pick = jnp.where(col == feature, 1.0, 0.0).astype(BF16)

    def window(ref):
        return lax.dot_general(pick, ref[:, :WINDOW], (((1,), (1,)), ((), ())), preferred_element_type=F32).astype(BF16)

    base[...] = jnp.full(base.shape, 1e-33, F32)
    blocks = part // 256

    def multiply(i, carry):
        own_copy(i).wait()
        other_copy(i).wait_recv()

        @pl.when(i == 0)
        def _():
            wt[:, :depth] = window(own)
            wt[:, depth:] = window(other)

        for j in range(blocks):
            b = i * blocks + j
            cols = pl.ds(pl.multiple_of(b * 256, 256), 256)
            product = jnp.dot(wt[:, :depth], own[:, cols], preferred_element_type=F32)
            product = product + jnp.dot(wt[:, depth:], other[:, cols], preferred_element_type=F32)
            bx, bz = b // NZ, lax.rem(b, NZ)
            prod[bx, bz, 0] = product[:, :128]
            prod[bx, bz, 1] = product[:, 128:]
            top = jnp.max(jnp.abs(product).reshape(UNITS, UNIT, 256), axis=0)
            base[...] = jnp.maximum(base[...], jnp.maximum(top[:, :128], top[:, 128:]))
        return carry

    lax.fori_loop(0, PIECES, multiply, 0)
    up_own.wait()
    up_other.wait_recv()

    count = len(ring_refs) // 4
    refs = [ring_refs[i * count:(i + 1) * count] for i in range(4)]
    along_z = lambda at: (y, (x * NZ + at) * 2 + c)
    along_x = lambda at: (y, (at * NZ + z) * 2 + c)
    rows = lambda u: pl.ds(pl.multiple_of(u * UNIT, UNIT), UNIT)
    az = Ring(*SHAPES[0], z, along_z, base, lambda dest, h, k: prod[:, dest, h, rows(k), :], refs[0])
    ax = Ring(*SHAPES[1], x, along_x, base_a, lambda dest, h, k: mid_a[k, h, pl.ds(dest, 1)], refs[1])
    bx = Ring(*SHAPES[2], x, along_x, base, lambda dest, h, k: prod[dest, :, h, rows(KA + k), :], refs[2])
    bz = Ring(*SHAPES[3], z, along_z, base_b, lambda dest, h, k: mid_b[k, h, pl.ds(dest, 1)], refs[3])

    def numerators(k):
        g = [jnp.concatenate([fin[k, 0, h], fin[k, 1, h]], axis=0) for h in (0, 1)]
        total = None
        for h in (0, 1):
            high = g[h].astype(BF16)
            low = (g[h] - high.astype(F32)).astype(BF16)
            term = jnp.dot(jnp.concatenate([high, low], axis=0), upv[h], preferred_element_type=F32)
            total = term if total is None else total + term
        total = total[:2 * UNIT] + total[2 * UNIT:]
        tiles = total.reshape(2 * UNIT, 8, 128)
        for p in range(NY):
            for half in (0, 1):
                for ab in (0, 1):
                    for i in (0, 1):
                        msg1[k, 2 * p + half, 2 * ab + i] = tiles[UNIT * ab + 4 * p + 2 * i + half]
                    msg1[k, 2 * p + half, 4, 4 * ab:4 * ab + 4, :] = fin[k, ab, half, 4 * p:4 * p + 4, :]

        def post(o, carry):
            pc, to = pair_of(o)
            pltpu.make_async_remote_copy(src_ref=msg1.at[k, pc], dst_ref=recv1.at[k, o - 1], send_sem=send1.at[k],
                                         recv_sem=sem1.at[k], device_id=to, device_id_type=MESH).start()
            return carry

        lax.fori_loop(1, 2 * NY, post, 0)

    def pair_copies(k):
        return pltpu.make_async_remote_copy(src_ref=recv1.at[k], dst_ref=recv1.at[k], send_sem=send1.at[k],
                                            recv_sem=sem1.at[k], device_id=sibling, device_id_type=MESH)

    def row_copy(src, to_chip):
        slot = lax.rem(to_chip - chip + CHIPS, CHIPS) - 1
        return pltpu.make_async_remote_copy(src_ref=src, dst_ref=recv2.at[slot], send_sem=send2, recv_sem=sem2,
                                            device_id=(y, to_chip * 2 + c), device_id_type=MESH)

    def pass_on(k):
        pair_copies(k).wait_recv()
        total = msg1[k, y * 2 + c]
        for o in range(2 * NY - 1):
            total = total + recv1[k, o]
        msg2[k] = total[:4]
        gacc[k] = total[4]
        for ab in (0, 1):

            @pl.when(k < (KA, KB)[ab])
            def _():
                for i in (0, 1):
                    u = k + ab * KA
                    to = (u // 4) * NZ + 2 * lax.rem(u, 4) + i

                    @pl.when(to == chip)
                    def _():
                        recv2[CHIPS - 1] = msg2[k, 2 * ab + i]

                    @pl.when(to != chip)
                    def _():
                        row_copy(msg2.at[k, 2 * ab + i], to).start()

    def put(ref, k):
        def store(h, value):
            ref[k, h] = value
        return store

    def put_final(ab, k):
        def store(h, value):
            fin[k, ab, h] = value[0] * scale
        return store

    for k in range(KA, K):
        fin[k, 0] = jnp.zeros(fin.shape[2:], F32)

    def when(k, units, run):
        pl.when(jnp.logical_and(k >= 0, k < units))(lambda: run(k))

    def az_to_ax(k):
        az.finish(k, base_a, put(mid_a, k))
        ax.send(0, k)

    def bx_to_bz(k):
        bx.finish(k, base_b, put(mid_b, k))
        bz.send(0, k)

    def tick(at, carry):
        a = [functools.partial(az.send, s) for s in range(4)]
        a += [az_to_ax, functools.partial(ax.send, 1), lambda k: ax.finish(k, None, put_final(0, k))]
        b = [functools.partial(bx.send, s) for s in range(2)]
        b += [bx_to_bz] + [functools.partial(bz.send, s) for s in range(1, 4)]
        b += [lambda k: bz.finish(k, None, put_final(1, k))]
        for stage in range(7):
            when(at - stage, KA, a[stage])
            when(at - stage, KB, b[stage])
        when(at - 6, K, numerators)
        when(at - 7, K, pass_on)
        return carry

    lax.fori_loop(0, K + 8, tick, 0)

    for k in range(K):
        if k < KA:
            gram[4 * k:4 * k + 4, :] = gacc[k, 0:4, :]
        if k < KB:
            u = KA + k
            gram[4 * u:4 * u + 4, :] = gacc[k, 4:8, :]
    all_rows = pltpu.make_async_remote_copy(src_ref=recv2.at[pl.ds(0, CHIPS - 1)], dst_ref=recv2.at[pl.ds(0, CHIPS - 1)],
                                            send_sem=send2, recv_sem=sem2, device_id=sibling, device_id_type=MESH)
    all_rows.wait_recv()
    total = jnp.sum(recv2[...], axis=0)
    for i in range(8):
        num[0:1, 128 * i:128 * (i + 1)] = total[i:i + 1, :]

    all_rows.wait_send()
    for k in range(K):
        pair_copies(k).wait_send()
    for ring in (az, ax, bx, bz):
        ring.sent()
    up_other.wait_send()
    pltpu.make_async_remote_copy(src_ref=tokens.at[oc], dst_ref=other, send_sem=other_send, recv_sem=other_send,
                                 device_id=sibling, device_id_type=MESH).wait_send()


def body(tokens, up_panel):
    variants, depth, width = tokens.shape
    block, panel = up_panel.shape[1:]
    scale = 1.0 / (depth * lax.axis_size("tok"))
    dma = pltpu.SemaphoreType.DMA
    scratch = [
        pltpu.VMEM((depth, width), BF16),
        pltpu.VMEM((depth, width), BF16),
        pltpu.VMEM((WINDOW, 2 * depth), BF16),
        pltpu.VMEM((2, block, panel), BF16),
        pltpu.VMEM((NX, NZ, 2, WINDOW, 128), F32),
        pltpu.VMEM((UNIT, 128), F32),
        pltpu.VMEM((UNIT, 128), F32),
        pltpu.VMEM((UNIT, 128), F32),
        pltpu.VMEM((KA, 2, NX, UNIT, 128), F32),
        pltpu.VMEM((KB, 2, NZ, UNIT, 128), F32),
        pltpu.VMEM((K, 2, 2, UNIT, 128), F32),
        pltpu.VMEM((K, 2 * NY, 5, 8, 128), F32),
        pltpu.VMEM((K, 2 * NY - 1, 5, 8, 128), F32),
        pltpu.VMEM((K, 4, 8, 128), F32),
        pltpu.VMEM((CHIPS, 8, 128), F32),
        pltpu.VMEM((K, 8, 128), F32),
        dma((PIECES,)), dma, dma((PIECES,)), dma, dma, dma,
        dma((K,)), dma((K,)), dma, dma,
    ]
    for shape in SHAPES:
        scratch += Ring.scratch(*shape)
    gram, num = pl.pallas_call(
        functools.partial(kernel, scale),
        out_shape=(
            jax.ShapeDtypeStruct((WINDOW // NY, block), F32),
            jax.ShapeDtypeStruct((1, panel), F32),
        ),
        in_specs=[pl.BlockSpec(memory_space=pl.ANY)] * 2,
        out_specs=(pl.BlockSpec(memory_space=pltpu.VMEM),) * 2,
        scratch_shapes=scratch,
        compiler_params=pltpu.CompilerParams(
            collective_id=0, has_side_effects=True, vmem_limit_bytes=60 * 2**20
        ),
    )(tokens, up_panel)
    return gram, num


def solution(mesh):
    return jax.shard_map(
        body,
        mesh=mesh,
        in_specs=(P("var", "tok", None), P("var", "tok", None)),
        out_specs=(P("var", "tok"), P(("var", "tok"), None)),
        check_vma=False,
    )
```

time: 503 us -> 78.4 us (0.16)
  waiting for transfers between devices: 471 us -> 0 us
  Pallas kernels: 0 us -> 74.9 us
  matrix products: 13.2 us -> 0 us
  between operations: 13.8 us -> 0.64 us
    unnamed x4 -> x0, waiting for transfers between devices: 259 us -> none
    reduce_scatter x2 -> x0, waiting for transfers between devices: 212 us -> none  [the longest x1 189 us: body(): lax.psum_scatter(product.reshape(block * lax.axis_size('tok'), var_count...]
    pallas_call x0 -> x1, Pallas kernels: none -> 74.9 us  [body(): pl.pallas_call(functools.partial(kernel, scale), out_shape=(jax.ShapeDtyp...]
    dot_general x2 -> x0, matrix products: 13.2 us -> none  [the longest x1 11.6 us: body(): jnp.einsum('vtc,vtg->cvg', tokens, window, preferred_element_type=jnp.flo...]
  transfers between devices with their start and end apart: 3 -> 0, of which waited for: 3 -> 0; matrix products, arithmetic and copies ran while one was open for 0% -> 0% of each run, Pallas kernels for 0% -> 0%
where the time goes in v1:
time: 78.4 us; the launch traced here: 78.2 us
  Pallas kernels  74.9 us (96%)
  local copies, waits for them, and re-layouts  2.65 us (3%)
    pallas_call x1, Pallas kernels, body(): pl.pallas_call(functools.partial(kernel, scale), out_shape=(jax.ShapeDtyp...  74.9 us
    unnamed x2, local copies, waits for them, and re-layouts  2.65 us

profile of v1, /device:TPU:1, one launch (start us, length us, event | category | flops | bytes accessed | tf_op | source)
XLA Modules:
  0.0 78.2 jit_solution(6619003944857206)
XLA Ops:
  0.6 74.9 %shard_map.41 = (f32[64,128]{1,0:T(8,128)}, f32[1,1024]{1,0:T(1,128)}) custom-call(bf16[2,256,8192]{2,1,0:T(8,128)(2,1)} %tokens.1, bf16[2,128,1024]{2,1,0:T(8,128)(2,1)} %up.1), custom_call_target="tpu_custom_call" | custom-call | tf_op jit(solution)/shard_map/pallas_call | solution.py:383
  75.5 1.4 %copy.6 = f32[64,128]{1,0:T(8,128)} copy(f32[64,128]{1,0:T(8,128)} %get-tuple-element.4) | data formatting | bytes 65536
  76.9 1.3 %copy.7 = f32[1,1024]{1,0:T(1,128)} copy(f32[1,1024]{1,0:T(1,128)} %get-tuple-element.5) | data formatting | bytes 8192

commit v2 on v1

v2 whole, which is shorter than its diff:
```python
import functools

import jax
import jax.numpy as jnp
from jax import lax
from jax.experimental import pallas as pl
from jax.experimental.pallas import tpu as pltpu
from jax.sharding import PartitionSpec as P

WINDOW = 256
NX, NZ, NY = 4, 8, 4
CHIPS = NX * NZ
UNIT = 16
UNITS = WINDOW // UNIT
KA = 6
KB = UNITS - KA
PAIRS = UNITS // 2
POWER = 9
TOP = 2.0**13.8
MESH = pl.DeviceIdType.MESH
F32, BF16 = jnp.float32, jnp.bfloat16


def encode(value, factor):
    t = value * factor
    t2 = t * t
    t4 = t2 * t2
    return (t4 * t4 * t).astype(BF16)


def decode(code, factor):
    y = code.astype(F32)
    root = jnp.exp2(jnp.log(jnp.maximum(jnp.abs(y), 1e-38)) * (1.4426950408889634 / POWER))
    return jnp.where(y < 0, -root, root) * factor


class Ring:
    def __init__(self, n, blocks, units, me, device, base, source, refs):
        self.n, self.half, self.units = n, n // 2, units
        self.me, self.device, self.base, self.source = me, device, base, source
        (self.s0, self.sn, self.r0, self.rn, self.bs, self.br, self.enc, self.dec,
         self.send_sem, self.recv_sem, self.bsend_sem, self.brecv_sem) = refs

    @staticmethod
    def scratch(n, blocks, units):
        half = n // 2
        first = pltpu.VMEM((units, 2, blocks, UNIT, 128), BF16)
        later = pltpu.VMEM((units, 2, half - 1, 2, blocks, UNIT, 128), BF16)
        bound = pltpu.VMEM((2, half, UNIT, 128), F32)
        return [first, later, first, later, bound, bound, bound, bound,
                pltpu.SemaphoreType.DMA((2,)), pltpu.SemaphoreType.DMA((units, 2, half)),
                pltpu.SemaphoreType.DMA, pltpu.SemaphoreType.DMA((2, half))]

    def data_copy(self, k, d, s, to):
        if s == 0:
            src, dst = self.s0.at[k, d], self.r0.at[k, d]
        else:
            src, dst = self.sn.at[k, d, s - 1], self.rn.at[k, d, s - 1]
        return pltpu.make_async_remote_copy(
            src_ref=src, dst_ref=dst, send_sem=self.send_sem.at[min(s, 1)],
            recv_sem=self.recv_sem.at[k, d, s], device_id=to, device_id_type=MESH)

    def bound_copy(self, d, s, to):
        return pltpu.make_async_remote_copy(
            src_ref=self.bs.at[d, s], dst_ref=self.br.at[d, s], send_sem=self.bsend_sem,
            recv_sem=self.brecv_sem.at[d, s], device_id=to, device_id_type=MESH)

    def neighbour(self, d):
        return self.device(lax.rem(self.me + (1 if d == 0 else self.n - 1), self.n))

    def dest(self, d, s):
        far = self.half - s
        return lax.rem(self.me + (far if d == 0 else self.n - far), self.n)

    def bounds(self, s):
        for d in (0, 1):
            to = self.neighbour(d)
            bound = self.base[self.dest(d, s)]
            if s > 0:
                self.bound_copy(d, s - 1, to).wait_recv()
                came = self.br[d, s - 1]
                self.dec[d, s - 1] = came * (1.0 / TOP)
                bound = bound + came
            self.bs[d, s] = bound
            self.enc[d, s] = TOP / bound
            self.bound_copy(d, s, to).start()

    def send(self, s, k):
        for d in (0, 1):
            to = self.neighbour(d)
            dest = self.dest(d, s)
            enc = self.enc[d, s]
            if s == 0:
                self.s0[k, d] = encode(self.source(dest, d, k), enc)
            else:
                self.data_copy(k, d, s - 1, to).wait_recv()
                dec = self.dec[d, s - 1]
                for h in (0, 1):
                    value = self.source(dest, h, k)
                    if s > 1:
                        value = value + decode(self.rn[k, d, s - 2, h], dec)
                    elif h == d:
                        value = value + decode(self.r0[k, d], dec)
                    self.sn[k, d, s - 1, h] = encode(value, enc)
            self.data_copy(k, d, s, to).start()

    def last_bounds(self, total):
        last = self.half - 1
        for d in (0, 1):
            self.bound_copy(d, last, self.neighbour(d)).wait_recv()
            self.dec[d, last] = self.br[d, last] * (1.0 / TOP)
        total[...] = self.base[self.me] + self.br[0, last] + self.br[1, last]

    def finish(self, k, store):
        last = self.half - 1
        for d in (0, 1):
            self.data_copy(k, d, last, self.neighbour(d)).wait_recv()
        for h in (0, 1):
            value = self.source(self.me, h, k)
            for d in (0, 1):
                value = value + decode(self.rn[k, d, last - 1, h], self.dec[d, last])
            store(h, value)

    def sent(self):
        to = self.neighbour(0)
        for src, dst, sem in ((self.s0, self.r0, self.send_sem.at[0]), (self.sn, self.rn, self.send_sem.at[1]),
                              (self.bs, self.br, self.bsend_sem)):
            pltpu.make_async_remote_copy(src_ref=src, dst_ref=dst, send_sem=sem, recv_sem=sem,
                                         device_id=to, device_id_type=MESH).wait_send()


class Exchange:
    def __init__(self, n, units, me, device, mid, refs):
        self.n, self.units, self.me, self.device, self.mid = n, units, me, device, mid
        self.out, self.came, self.bound, self.bcame, self.send_sem, self.recv_sem, self.bsend_sem, self.brecv_sem = refs

    @staticmethod
    def scratch(n, units):
        return [pltpu.VMEM((units, n, 2, UNIT, 128), BF16), pltpu.VMEM((units, n - 1, 2, UNIT, 128), BF16),
                pltpu.VMEM((UNIT, 128), F32), pltpu.VMEM((n - 1, UNIT, 128), F32),
                pltpu.SemaphoreType.DMA((units,)), pltpu.SemaphoreType.DMA((units,)),
                pltpu.SemaphoreType.DMA, pltpu.SemaphoreType.DMA]

    def far(self, o):
        at = lax.rem(self.me + o, self.n)
        return at, self.device(at)

    def bounds(self):
        for o in range(1, self.n):
            pltpu.make_async_remote_copy(src_ref=self.bound, dst_ref=self.bcame.at[o - 1], send_sem=self.bsend_sem,
                                         recv_sem=self.brecv_sem, device_id=self.far(o)[1], device_id_type=MESH).start()

    def send(self, k):
        enc = TOP / self.bound[...]
        for h in (0, 1):
            self.out[k, :, h] = encode(self.mid[k, h], enc)
        for o in range(1, self.n):
            at, to = self.far(o)
            pltpu.make_async_remote_copy(src_ref=self.out.at[k, at], dst_ref=self.came.at[k, o - 1],
                                         send_sem=self.send_sem.at[k], recv_sem=self.recv_sem.at[k],
                                         device_id=to, device_id_type=MESH).start()

    def all_bounds(self):
        return pltpu.make_async_remote_copy(src_ref=self.bcame, dst_ref=self.bcame, send_sem=self.bsend_sem,
                                            recv_sem=self.brecv_sem, device_id=self.far(1)[1], device_id_type=MESH)

    def all_data(self, k):
        return pltpu.make_async_remote_copy(src_ref=self.came.at[k], dst_ref=self.came.at[k], send_sem=self.send_sem.at[k],
                                            recv_sem=self.recv_sem.at[k], device_id=self.far(1)[1], device_id_type=MESH)

    def finish(self, k, store):
        self.all_data(k).wait_recv()
        for h in (0, 1):
            value = self.mid[k, h, self.me]
            for o in range(self.n - 1):
                value = value + decode(self.came[k, o, h], self.bcame[o] * (1.0 / TOP))
            store(h, value)

    def sent(self):
        self.all_bounds().wait_send()
        for k in range(self.units):
            self.all_data(k).wait_send()


RINGS = ((NZ, NX, KA), (NX, NZ, KB))
EXCHANGES = ((NX, KA), (NZ, KB))


def kernel(scale, tokens, up, gram, num, own, other, wown, wother, wt, upv, prod, base_z, base_x, mid_a, mid_b, fin,
           msg1, recv1, msg2, recv2, gacc, own_sem, other_send, other_recv, up_sem, up_send, up_recv,
           send1, sem1, send2, sem2, met, *refs):
    y, t = lax.axis_index("var"), lax.axis_index("tok")
    c = lax.rem(t, 2)
    chip = t // 2
    z, x = lax.rem(chip, NZ), chip // NZ
    oc = 1 - c
    sibling = (y, chip * 2 + oc)
    depth = own.shape[0]
    along_z = lambda at: (y, (x * NZ + at) * 2 + c)
    along_x = lambda at: (y, (at * NZ + z) * 2 + c)
    rows = lambda u: pl.ds(pl.multiple_of(u * UNIT, UNIT), UNIT)

    parts = (
        (8, lambda i: (2, i)),
        (3, lambda i: (lax.rem(3 + i, 4), 4)),
        (6, lambda i: (lax.rem(3 + lax.rem(i, 3), 4), 3 + 2 * (i // 3))),
        (10, lambda i: (1 + 2 * (i // 5), lax.rem(6 + lax.rem(i, 5), 8))),
        (5, lambda i: (0, lax.rem(6 + i, 8))),
    )
    starts = [sum(p[0] for p in parts[:j]) for j in range(len(parts))]

    def block_at(part, i):
        dx, dz = parts[part][1](i)
        bx, bz = lax.rem(x + dx, NX), lax.rem(z + dz, NZ)
        return bx, bz, pl.ds(pl.multiple_of((bx * NZ + bz) * 256, 256), 256)

    def own_copy(cols, at):
        return pltpu.make_async_copy(tokens.at[c, :, cols], own.at[:, cols], own_sem.at[at])

    def other_copy(cols, at):
        return pltpu.make_async_remote_copy(
            src_ref=tokens.at[oc, :, cols], dst_ref=other.at[:, cols], send_sem=other_send,
            recv_sem=other_recv.at[at], device_id=sibling, device_id_type=MESH)

    def each_block(run):
        for part, (size, _) in enumerate(parts):
            def one(i, carry):
                run(block_at(part, i)[2], starts[part] + i)
                return carry
            lax.fori_loop(0, size, one, 0)

    front = pl.ds(0, WINDOW)
    wown_copy = pltpu.make_async_copy(tokens.at[c, :, front], wown, own_sem.at[CHIPS])
    wother_copy = pltpu.make_async_remote_copy(
        src_ref=tokens.at[oc, :, front], dst_ref=wother, send_sem=up_send.at[0], recv_sem=other_recv.at[CHIPS],
        device_id=sibling, device_id_type=MESH)
    up_own = pltpu.make_async_copy(up.at[c], upv.at[c], up_sem)
    up_other = pltpu.make_async_remote_copy(src_ref=up.at[oc], dst_ref=upv.at[c], send_sem=up_send.at[1],
                                            recv_sem=up_recv, device_id=sibling, device_id_type=MESH)

    barrier = pltpu.get_barrier_semaphore()
    peers = [sibling] + [along_z(lax.rem(z + o, NZ)) for o in (1, NZ - 1)]
    peers += [along_x(lax.rem(x + o, NX)) for o in (1, NX - 1)]
    over_y = [(lax.rem(y + o, NY), t) for o in range(1, NY)]
    for to in peers + over_y:
        pl.semaphore_signal(barrier, inc=1, device_id=to, device_id_type=MESH)
    wown_copy.start()
    each_block(lambda cols, at: own_copy(cols, at).start())
    up_own.start()

    row = lax.broadcasted_iota(jnp.int32, (WINDOW, WINDOW), 0)
    col = lax.broadcasted_iota(jnp.int32, (WINDOW, WINDOW), 1)
    feature = ((row >> 2) & 3) * (WINDOW // NY) + (row >> 4) * 4 + (row & 3)
    pick = jnp.where(col == feature, 1.0, 0.0).astype(BF16)

    def window(ref):
        return lax.dot_general(pick, ref[...], (((1,), (1,)), ((), ())), preferred_element_type=F32).astype(BF16)

    wown_copy.wait()
    wt[:, :depth] = window(wown)
    for ref in (base_z, base_x):
        ref[...] = jnp.full(ref.shape, 1e-33, F32)

    pl.semaphore_wait(barrier, len(peers) + len(over_y))
    wother_copy.start()
    each_block(lambda cols, at: other_copy(cols, at).start())
    up_other.start()
    for to in over_y:
        pl.semaphore_signal(met, inc=1, device_id=to, device_id_type=MESH)
    wother_copy.wait_recv()
    wt[:, depth:] = window(wother)

    def multiply(part):
        def one(i, carry):
            bx, bz, cols = block_at(part, i)
            at = starts[part] + i
            own_copy(cols, at).wait()
            other_copy(cols, at).wait_recv()
            product = jnp.dot(wt[:, :depth], own[:, cols], preferred_element_type=F32)
            product = product + jnp.dot(wt[:, depth:], other[:, cols], preferred_element_type=F32)
            prod[bx, bz, 0] = product[:, :128]
            prod[bx, bz, 1] = product[:, 128:]
            top = jnp.max(jnp.abs(product).reshape(UNITS, UNIT, 256), axis=0)
            top = jnp.maximum(top[:, :128], top[:, 128:])
            base_z[bz] = jnp.maximum(base_z[bz], top)
            base_x[bx] = jnp.maximum(base_x[bx], top)
            return carry
        lax.fori_loop(0, parts[part][0], one, 0)

    sizes = (12, 12, 8, 8)
    split = [refs[sum(sizes[:j]):sum(sizes[:j + 1])] for j in range(4)]
    az = Ring(*RINGS[0], z, along_z, base_z, lambda dest, h, k: prod[:, dest, h, rows(k), :], split[0])
    bx = Ring(*RINGS[1], x, along_x, base_x, lambda dest, h, k: prod[dest, :, h, rows(KA + k), :], split[1])
    ax = Exchange(*EXCHANGES[0], x, along_x, mid_a, split[2])
    bz = Exchange(*EXCHANGES[1], z, along_z, mid_b, split[3])

    def pair_of(o):
        pc = lax.rem(y * 2 + c + o, 2 * NY)
        return pc, (pc // 2, chip * 2 + lax.rem(pc, 2))

    def numerators(j):
        total = None
        for h in (0, 1):
            g = jnp.concatenate([fin[2 * j, h], fin[2 * j + 1, h]], axis=0)
            high = g.astype(BF16)
            low = (g - high.astype(F32)).astype(BF16)
            term = jnp.dot(jnp.concatenate([high, low], axis=0), upv[h], preferred_element_type=F32)
            total = term if total is None else total + term
        total = total[:2 * UNIT] + total[2 * UNIT:]
        tiles = total.reshape(2 * UNIT, 8, 128)
        for p in range(NY):
            for half in (0, 1):
                for ab in (0, 1):
                    for i in (0, 1):
                        msg1[j, 2 * p + half, 2 * ab + i] = tiles[UNIT * ab + 4 * p + 2 * i + half]
                    msg1[j, 2 * p + half, 4, 4 * ab:4 * ab + 4, :] = fin[2 * j + ab, half, 4 * p:4 * p + 4, :]

        def post(o, carry):
            pc, to = pair_of(o)
            pltpu.make_async_remote_copy(src_ref=msg1.at[j, pc], dst_ref=recv1.at[j, o - 1], send_sem=send1.at[j],
                                         recv_sem=sem1.at[j], device_id=to, device_id_type=MESH).start()
            return carry

        lax.fori_loop(1, 2 * NY, post, 0)

    def pair_copies(j):
        return pltpu.make_async_remote_copy(src_ref=recv1.at[j], dst_ref=recv1.at[j], send_sem=send1.at[j],
                                            recv_sem=sem1.at[j], device_id=sibling, device_id_type=MESH)

    def row_copy(src, to_chip):
        slot = lax.rem(to_chip - chip + CHIPS, CHIPS) - 1
        return pltpu.make_async_remote_copy(src_ref=src, dst_ref=recv2.at[slot], send_sem=send2, recv_sem=sem2,
                                            device_id=(y, to_chip * 2 + c), device_id_type=MESH)

    def pass_on(j):
        pair_copies(j).wait_recv()
        total = msg1[j, y * 2 + c]
        for o in range(2 * NY - 1):
            total = total + recv1[j, o]
        msg2[j] = total[:4]
        gacc[j] = total[4]

        def row_out(i, carry):
            u = 2 * j + i // 2
            to = (u // 4) * NZ + 2 * lax.rem(u, 4) + lax.rem(i, 2)

            @pl.when(to == chip)
            def _():
                recv2[CHIPS - 1] = msg2[j, i]

            @pl.when(to != chip)
            def _():
                row_copy(msg2.at[j, i], to).start()
            return carry

        lax.fori_loop(0, 4, row_out, 0)

    def run(step, low, high):
        def one(k, carry):
            step(k)
            return carry
        lax.fori_loop(low, high, one, 0)

    def put(ref, k):
        def store(h, value):
            ref[k, h] = value
        return store

    def put_final(u):
        def store(h, value):
            fin[u, h] = value * scale
        return store

    def a_turn(k):
        az.finish(k, put(mid_a, k))
        ax.send(k)

    def b_turn(k):
        bx.finish(k, put(mid_b, k))
        bz.send(k)

    def a_pair(j):
        for i in (0, 1):
            ax.finish(2 * j + i, put_final(2 * j + i))
        numerators(j)

    def b_pair(j):
        for i in (0, 1):
            bz.finish(2 * j + i, put_final(KA + 2 * j + i))
        numerators(KA // 2 + j)

    a_send = lambda s: functools.partial(az.send, s)
    b_send = lambda s: functools.partial(bx.send, s)
    half_b = KB // 2
    multiply(0)
    multiply(1)
    az.bounds(0)
    run(a_send(0), 0, KA)
    bx.bounds(0)
    run(b_send(0), 0, KB)
    multiply(2)
    az.bounds(1)
    run(a_send(1), 0, KA)
    multiply(3)
    bx.bounds(1)
    run(b_send(1), 0, half_b)
    multiply(4)
    az.bounds(2)
    run(a_send(2), 0, KA)
    run(b_send(1), half_b, KB)
    az.bounds(3)
    run(a_send(3), 0, KA)
    bx.last_bounds(bz.bound)
    az.last_bounds(ax.bound)
    bz.bounds()
    ax.bounds()
    run(b_turn, 0, 3)
    run(a_turn, 0, KA)
    run(b_turn, 3, KB - 3)
    up_own.wait()
    up_other.wait_recv()
    pl.semaphore_wait(met, NY - 1)
    ax.all_bounds().wait_recv()
    run(a_pair, 0, KA // 2)
    run(b_turn, KB - 3, KB)
    bz.all_bounds().wait_recv()
    run(pass_on, 0, KA // 2)
    b_pair(0)

    def b_step(j):
        b_pair(j)
        pass_on(KA // 2 + j - 1)

    run(b_step, 1, KB // 2)
    pass_on(PAIRS - 1)

    for u in range(UNITS):
        gram[4 * u:4 * u + 4, :] = gacc[u // 2, 4 * (u % 2):4 * (u % 2) + 4, :]
    all_rows = pltpu.make_async_remote_copy(src_ref=recv2.at[pl.ds(0, CHIPS - 1)], dst_ref=recv2.at[pl.ds(0, CHIPS - 1)],
                                            send_sem=send2, recv_sem=sem2, device_id=sibling, device_id_type=MESH)
    all_rows.wait_send()
    for j in range(PAIRS):
        pair_copies(j).wait_send()
    for group in (az, bx, ax, bz):
        group.sent()
    wother_copy.wait_send()
    up_other.wait_send()
    pltpu.make_async_remote_copy(src_ref=tokens.at[oc], dst_ref=other, send_sem=other_send, recv_sem=other_send,
                                 device_id=sibling, device_id_type=MESH).wait_send()
    all_rows.wait_recv()
    total = jnp.sum(recv2[...], axis=0)
    for i in range(8):
        num[0:1, 128 * i:128 * (i + 1)] = total[i:i + 1, :]


def body(tokens, up_panel):
    variants, depth, width = tokens.shape
    block, panel = up_panel.shape[1:]
    scale = 1.0 / (depth * lax.axis_size("tok"))
    dma = pltpu.SemaphoreType.DMA
    scratch = [
        pltpu.VMEM((depth, width), BF16),
        pltpu.VMEM((depth, width), BF16),
        pltpu.VMEM((depth, WINDOW), BF16),
        pltpu.VMEM((depth, WINDOW), BF16),
        pltpu.VMEM((WINDOW, 2 * depth), BF16),
        pltpu.VMEM((2, block, panel), BF16),
        pltpu.VMEM((NX, NZ, 2, WINDOW, 128), F32),
        pltpu.VMEM((NZ, UNIT, 128), F32),
        pltpu.VMEM((NX, UNIT, 128), F32),
        pltpu.VMEM((KA, 2, NX, UNIT, 128), F32),
        pltpu.VMEM((KB, 2, NZ, UNIT, 128), F32),
        pltpu.VMEM((UNITS, 2, UNIT, 128), F32),
        pltpu.VMEM((PAIRS, 2 * NY, 5, 8, 128), F32),
        pltpu.VMEM((PAIRS, 2 * NY - 1, 5, 8, 128), F32),
        pltpu.VMEM((PAIRS, 4, 8, 128), F32),
        pltpu.VMEM((CHIPS, 8, 128), F32),
        pltpu.VMEM((PAIRS, 8, 128), F32),
        dma((CHIPS + 1,)), dma, dma((CHIPS + 1,)), dma, dma((2,)), dma,
        dma((PAIRS,)), dma((PAIRS,)), dma, dma, pltpu.SemaphoreType.REGULAR,
    ]
    for shape in RINGS:
        scratch += Ring.scratch(*shape)
    for shape in EXCHANGES:
        scratch += Exchange.scratch(*shape)
    gram, num = pl.pallas_call(
        functools.partial(kernel, scale),
        out_shape=(
            jax.ShapeDtypeStruct((WINDOW // NY, block), F32),
            jax.ShapeDtypeStruct((1, panel), F32),
        ),
        in_specs=[pl.BlockSpec(memory_space=pl.ANY)] * 2,
        out_specs=(pl.BlockSpec(memory_space=pltpu.VMEM),) * 2,
        scratch_shapes=scratch,
        compiler_params=pltpu.CompilerParams(
            collective_id=0, has_side_effects=True, vmem_limit_bytes=60 * 2**20
        ),
    )(tokens, up_panel)
    return gram, num


def solution(mesh):
    return jax.shard_map(
        body,
        mesh=mesh,
        in_specs=(P("var", "tok", None), P("var", "tok", None)),
        out_specs=(P("var", "tok"), P(("var", "tok"), None)),
        check_vma=False,
    )
```

time: 78.4 us -> 69.4 us (0.89)
  Pallas kernels: 74.9 us -> 65.9 us
    pallas_call x1, Pallas kernels: 74.9 us -> 65.9 us  [body(): pl.pallas_call(functools.partial(kernel, scale), out_shape=(jax.ShapeDtyp...]
where the time goes in v2:
time: 69.4 us; the launch traced here: 69.2 us
  Pallas kernels  65.9 us (95%)
  local copies, waits for them, and re-layouts  2.65 us (4%)
    pallas_call x1, Pallas kernels, body(): pl.pallas_call(functools.partial(kernel, scale), out_shape=(jax.ShapeDtyp...  65.9 us
    unnamed x2, local copies, waits for them, and re-layouts  2.65 us

profile of v2, /device:TPU:1, one launch (start us, length us, event | category | flops | bytes accessed | tf_op | source)
XLA Modules:
  0.0 69.2 jit_solution(12605778709137489839)
XLA Ops:
  0.6 65.9 %shard_map.41 = (f32[64,128]{1,0:T(8,128)}, f32[1,1024]{1,0:T(1,128)}) custom-call(bf16[2,256,8192]{2,1,0:T(8,128)(2,1)} %tokens.1, bf16[2,128,1024]{2,1,0:T(8,128)(2,1)} %up.1), custom_call_target="tpu_custom_call" | custom-call | tf_op jit(solution)/shard_map/pallas_call | solution.py:486
  66.6 1.4 %copy.6 = f32[64,128]{1,0:T(8,128)} copy(f32[64,128]{1,0:T(8,128)} %get-tuple-element.4) | data formatting | bytes 65536
  67.9 1.3 %copy.7 = f32[1,1024]{1,0:T(1,128)} copy(f32[1,1024]{1,0:T(1,128)} %get-tuple-element.5) | data formatting | bytes 8192

commit v3 on v2

--- a/solution.py
+++ b/solution.py
@@ -15,6 +15,7 @@
 KA = 6
 KB = UNITS - KA
 PAIRS = UNITS // 2
+A2, A3, AT, BT, BE, AP, BP = 1, 5, 9, 5, 7, 14, 11
 POWER = 9
 TOP = 2.0**13.8
 MESH = pl.DeviceIdType.MESH
@@ -182,13 +183,88 @@
             self.all_data(k).wait_send()
 
 
+class HalfExchange(Exchange):
+    def __init__(self, n, units, me, device, mid, refs):
+        super().__init__(n, units, me, device, mid, refs[:8])
+        self.half = n // 2
+        self.pre, self.got, self.near, self.total, self.pre_send, self.pre_recv, self.near_send, self.near_recv = refs[8:]
+        self.others = [o for o in range(1, n) if o != self.half]
+
+    @staticmethod
+    def scratch(n, units):
+        dma = pltpu.SemaphoreType.DMA
+        piece = pltpu.VMEM((units, 2, UNIT, 128), BF16)
+        return [pltpu.VMEM((units, n, 2, UNIT, 128), BF16), pltpu.VMEM((units, n - 2, 2, UNIT, 128), BF16),
+                pltpu.VMEM((UNIT, 128), F32), pltpu.VMEM((n - 2, UNIT, 128), F32),
+                dma((units,)), dma((units,)), dma, dma,
+                piece, piece, pltpu.VMEM((2, UNIT, 128), F32), pltpu.VMEM((UNIT, 128), F32),
+                dma, dma((units, 2)), dma, dma((2,))]
+
+    def near_copy(self, d):
+        to = self.far(1 if d == 0 else self.n - 1)[1]
+        return pltpu.make_async_remote_copy(src_ref=self.bound, dst_ref=self.near.at[d], send_sem=self.near_send,
+                                            recv_sem=self.near_recv.at[d], device_id=to, device_id_type=MESH)
+
+    def pre_copy(self, k, d):
+        to = self.far(1 if d == 0 else self.n - 1)[1]
+        return pltpu.make_async_remote_copy(src_ref=self.pre.at[k, d], dst_ref=self.got.at[k, d], send_sem=self.pre_send,
+                                            recv_sem=self.pre_recv.at[k, d], device_id=to, device_id_type=MESH)
+
+    def near_bounds(self):
+        for d in (0, 1):
+            self.near_copy(d).start()
+
+    def first(self, k):
+        enc = TOP / self.bound[...]
+        for d in (0, 1):
+            self.pre[k, d] = encode(self.mid[k, d, self.far(self.half)[0]], enc)
+            self.pre_copy(k, d).start()
+
+    def bounds(self):
+        for d in (0, 1):
+            self.near_copy(d).wait_recv()
+        self.total[...] = self.bound[...] + self.near[0] + self.near[1]
+        for slot, o in enumerate(self.others):
+            pltpu.make_async_remote_copy(src_ref=self.total, dst_ref=self.bcame.at[slot], send_sem=self.bsend_sem,
+                                         recv_sem=self.brecv_sem, device_id=self.far(o)[1], device_id_type=MESH).start()
+
+    def send(self, k):
+        for d in (0, 1):
+            self.pre_copy(k, d).wait_recv()
+            at = self.far(self.half - 1 if d == 0 else self.half + 1)[0]
+            self.mid[k, d, at] = self.mid[k, d, at] + decode(self.got[k, d], self.near[d] * (1.0 / TOP))
+        enc = TOP / self.total[...]
+        for h in (0, 1):
+            self.out[k, :, h] = encode(self.mid[k, h], enc)
+        for slot, o in enumerate(self.others):
+            at, to = self.far(o)
+            pltpu.make_async_remote_copy(src_ref=self.out.at[k, at], dst_ref=self.came.at[k, slot],
+                                         send_sem=self.send_sem.at[k], recv_sem=self.recv_sem.at[k],
+                                         device_id=to, device_id_type=MESH).start()
+
+    def finish(self, k, store):
+        self.all_data(k).wait_recv()
+        for h in (0, 1):
+            value = self.mid[k, h, self.me]
+            for slot in range(self.n - 2):
+                value = value + decode(self.came[k, slot, h], self.bcame[slot] * (1.0 / TOP))
+            store(h, value)
+
+    def sent(self):
+        super().sent()
+        to = self.far(1)[1]
+        for src, dst, sem in ((self.pre, self.got, self.pre_send), (self.near, self.near, self.near_send)):
+            pltpu.make_async_remote_copy(src_ref=src, dst_ref=dst, send_sem=sem, recv_sem=sem,
+                                         device_id=to, device_id_type=MESH).wait_send()
+
+
 RINGS = ((NZ, NX, KA), (NX, NZ, KB))
 EXCHANGES = ((NX, KA), (NZ, KB))
 
 
 def kernel(scale, tokens, up, gram, num, own, other, wown, wother, wt, upv, prod, base_z, base_x, mid_a, mid_b, fin,
-           msg1, recv1, msg2, recv2, gacc, own_sem, other_send, other_recv, up_sem, up_send, up_recv,
-           send1, sem1, send2, sem2, met, *refs):
+           msg1, joined, recv1, msg2, recv2, gacc, own_sem, other_send, other_recv, up_sem, up_send, up_recv,
+           send0, sem0, send1, sem1, send2, sem2, *refs):
     y, t = lax.axis_index("var"), lax.axis_index("tok")
     c = lax.rem(t, 2)
     chip = t // 2
@@ -265,8 +341,6 @@
     wother_copy.start()
     each_block(lambda cols, at: other_copy(cols, at).start())
     up_other.start()
-    for to in over_y:
-        pl.semaphore_signal(met, inc=1, device_id=to, device_id_type=MESH)
     wother_copy.wait_recv()
     wt[:, depth:] = window(wother)
 
@@ -287,16 +361,12 @@
             return carry
         lax.fori_loop(0, parts[part][0], one, 0)
 
-    sizes = (12, 12, 8, 8)
+    sizes = (12, 12, 8, 16)
     split = [refs[sum(sizes[:j]):sum(sizes[:j + 1])] for j in range(4)]
     az = Ring(*RINGS[0], z, along_z, base_z, lambda dest, h, k: prod[:, dest, h, rows(k), :], split[0])
     bx = Ring(*RINGS[1], x, along_x, base_x, lambda dest, h, k: prod[dest, :, h, rows(KA + k), :], split[1])
     ax = Exchange(*EXCHANGES[0], x, along_x, mid_a, split[2])
-    bz = Exchange(*EXCHANGES[1], z, along_z, mid_b, split[3])
-
-    def pair_of(o):
-        pc = lax.rem(y * 2 + c + o, 2 * NY)
-        return pc, (pc // 2, chip * 2 + lax.rem(pc, 2))
+    bz = HalfExchange(*EXCHANGES[1], z, along_z, mid_b, split[3])
 
     def numerators(j):
         total = None
@@ -312,16 +382,22 @@
             for half in (0, 1):
                 for ab in (0, 1):
                     for i in (0, 1):
-                        msg1[j, 2 * p + half, 2 * ab + i] = tiles[UNIT * ab + 4 * p + 2 * i + half]
-                    msg1[j, 2 * p + half, 4, 4 * ab:4 * ab + 4, :] = fin[2 * j + ab, half, 4 * p:4 * p + 4, :]
-
-        def post(o, carry):
-            pc, to = pair_of(o)
-            pltpu.make_async_remote_copy(src_ref=msg1.at[j, pc], dst_ref=recv1.at[j, o - 1], send_sem=send1.at[j],
-                                         recv_sem=sem1.at[j], device_id=to, device_id_type=MESH).start()
-            return carry
-
-        lax.fori_loop(1, 2 * NY, post, 0)
+                        msg1[j, half, p, 2 * ab + i] = tiles[UNIT * ab + 4 * p + 2 * i + half]
+                    msg1[j, half, p, 4, 4 * ab:4 * ab + 4, :] = fin[2 * j + ab, half, 4 * p:4 * p + 4, :]
+        core_copy(j).start()
+
+    def core_copy(j):
+        return pltpu.make_async_remote_copy(src_ref=msg1.at[j, oc], dst_ref=joined.at[j], send_sem=send0.at[j],
+                                            recv_sem=sem0.at[j], device_id=sibling, device_id_type=MESH)
+
+    def join(j):
+        core_copy(j).wait_recv()
+        for p in range(NY):
+            msg1[j, c, p] = msg1[j, c, p] + joined[j, p]
+        for o in range(1, NY):
+            p = lax.rem(y + o, NY)
+            pltpu.make_async_remote_copy(src_ref=msg1.at[j, c, p], dst_ref=recv1.at[j, o - 1], send_sem=send1.at[j],
+                                         recv_sem=sem1.at[j], device_id=(p, t), device_id_type=MESH).start()
 
     def pair_copies(j):
         return pltpu.make_async_remote_copy(src_ref=recv1.at[j], dst_ref=recv1.at[j], send_sem=send1.at[j],
@@ -334,8 +410,8 @@
 
     def pass_on(j):
         pair_copies(j).wait_recv()
-        total = msg1[j, y * 2 + c]
-        for o in range(2 * NY - 1):
+        total = msg1[j, c, y]
+        for o in range(NY - 1):
             total = total + recv1[j, o]
         msg2[j] = total[:4]
         gacc[j] = total[4]
@@ -377,7 +453,7 @@
 
     def b_turn(k):
         bx.finish(k, put(mid_b, k))
-        bz.send(k)
+        bz.first(k)
 
     def a_pair(j):
         for i in (0, 1):
@@ -389,9 +465,31 @@
             bz.finish(2 * j + i, put_final(KA + 2 * j + i))
         numerators(KA // 2 + j)
 
+    def at_tick(at, start, count, step, prepare=None):
+        def now():
+            if prepare is not None:
+                pl.when(at == start)(prepare)
+            step(at - start)
+        pl.when(jnp.logical_and(at >= start, at < start + count))(now)
+
+    def two(step):
+        return lambda m: run(step, 2 * m, 2 * m + 2)
+
+    def every_other(step):
+        return lambda m: pl.when(lax.rem(m, 2) == 0)(lambda: step(m // 2))
+
     a_send = lambda s: functools.partial(az.send, s)
     b_send = lambda s: functools.partial(bx.send, s)
-    half_b = KB // 2
+    half_a, half_b = KA // 2, KB // 2
+
+    def a_meet():
+        az.last_bounds(ax.bound)
+        ax.bounds()
+
+    def b_meet():
+        bx.last_bounds(bz.bound)
+        bz.near_bounds()
+
     multiply(0)
     multiply(1)
     az.bounds(0)
@@ -403,36 +501,26 @@
     run(a_send(1), 0, KA)
     multiply(3)
     bx.bounds(1)
-    run(b_send(1), 0, half_b)
+    b_send(1)(0)
     multiply(4)
-    az.bounds(2)
-    run(a_send(2), 0, KA)
-    run(b_send(1), half_b, KB)
-    az.bounds(3)
-    run(a_send(3), 0, KA)
-    bx.last_bounds(bz.bound)
-    az.last_bounds(ax.bound)
-    bz.bounds()
-    ax.bounds()
-    run(b_turn, 0, 3)
-    run(a_turn, 0, KA)
-    run(b_turn, 3, KB - 3)
     up_own.wait()
     up_other.wait_recv()
-    pl.semaphore_wait(met, NY - 1)
-    ax.all_bounds().wait_recv()
-    run(a_pair, 0, KA // 2)
-    run(b_turn, KB - 3, KB)
-    bz.all_bounds().wait_recv()
-    run(pass_on, 0, KA // 2)
-    b_pair(0)
-
-    def b_step(j):
-        b_pair(j)
-        pass_on(KA // 2 + j - 1)
-
-    run(b_step, 1, KB // 2)
-    pass_on(PAIRS - 1)
+
+    def tick(at, carry):
+        at_tick(at, A2, half_a, two(a_send(2)), lambda: az.bounds(2))
+        at_tick(at, A3, half_a, two(a_send(3)), lambda: az.bounds(3))
+        at_tick(at, 1, KB - 1, lambda k: bx.send(1, k + 1))
+        at_tick(at, AT, half_a, two(a_turn), a_meet)
+        at_tick(at, BT, KB, b_turn, b_meet)
+        at_tick(at, BE, KB, bz.send, bz.bounds)
+        at_tick(at, AP, half_a, a_pair, lambda: ax.all_bounds().wait_recv())
+        at_tick(at, BP, KB - 1, every_other(b_pair), lambda: bz.all_bounds().wait_recv())
+        at_tick(at, AP + 1, half_a, join)
+        at_tick(at, BP + 1, KB - 1, every_other(lambda j: join(half_a + j)))
+        return carry
+
+    lax.fori_loop(0, BP + KB, tick, 0)
+    run(pass_on, 0, PAIRS)
 
     for u in range(UNITS):
         gram[4 * u:4 * u + 4, :] = gacc[u // 2, 4 * (u % 2):4 * (u % 2) + 4, :]
@@ -441,6 +529,7 @@
     all_rows.wait_send()
     for j in range(PAIRS):
         pair_copies(j).wait_send()
+        core_copy(j).wait_send()
     for group in (az, bx, ax, bz):
         group.sent()
     wother_copy.wait_send()
@@ -471,18 +560,18 @@
         pltpu.VMEM((KA, 2, NX, UNIT, 128), F32),
         pltpu.VMEM((KB, 2, NZ, UNIT, 128), F32),
         pltpu.VMEM((UNITS, 2, UNIT, 128), F32),
-        pltpu.VMEM((PAIRS, 2 * NY, 5, 8, 128), F32),
-        pltpu.VMEM((PAIRS, 2 * NY - 1, 5, 8, 128), F32),
+        pltpu.VMEM((PAIRS, 2, NY, 5, 8, 128), F32),
+        pltpu.VMEM((PAIRS, NY, 5, 8, 128), F32),
+        pltpu.VMEM((PAIRS, NY - 1, 5, 8, 128), F32),
         pltpu.VMEM((PAIRS, 4, 8, 128), F32),
         pltpu.VMEM((CHIPS, 8, 128), F32),
         pltpu.VMEM((PAIRS, 8, 128), F32),
         dma((CHIPS + 1,)), dma, dma((CHIPS + 1,)), dma, dma((2,)), dma,
-        dma((PAIRS,)), dma((PAIRS,)), dma, dma, pltpu.SemaphoreType.REGULAR,
+        dma((PAIRS,)), dma((PAIRS,)), dma((PAIRS,)), dma((PAIRS,)), dma, dma,
     ]
     for shape in RINGS:
         scratch += Ring.scratch(*shape)
-    for shape in EXCHANGES:
-        scratch += Exchange.scratch(*shape)
+    scratch += Exchange.scratch(*EXCHANGES[0]) + HalfExchange.scratch(*EXCHANGES[1])
     gram, num = pl.pallas_call(
         functools.partial(kernel, scale),
         out_shape=(

time: 69.4 us -> 63.1 us (0.909)
  Pallas kernels: 65.9 us -> 59.6 us
    pallas_call x1, Pallas kernels: 65.9 us -> 59.6 us  [body(): pl.pallas_call(functools.partial(kernel, scale), out_shape=(jax.ShapeDtyp...]
where the time goes in v3:
time: 63.1 us; the launch traced here: 62.9 us
  Pallas kernels  59.6 us (94%)
  local copies, waits for them, and re-layouts  2.65 us (4%)
  between operations  0.64 us (1%)
    pallas_call x1, Pallas kernels, body(): pl.pallas_call(functools.partial(kernel, scale), out_shape=(jax.ShapeDtyp...  59.6 us
    unnamed x2, local copies, waits for them, and re-layouts  2.65 us

profile of v3, /device:TPU:1, one launch (start us, length us, event | category | flops | bytes accessed | tf_op | source)
XLA Modules:
  0.0 62.9 jit_solution(15804393830115198021)
XLA Ops:
  0.6 59.6 %shard_map.41 = (f32[64,128]{1,0:T(8,128)}, f32[1,1024]{1,0:T(1,128)}) custom-call(bf16[2,256,8192]{2,1,0:T(8,128)(2,1)} %tokens.1, bf16[2,128,1024]{2,1,0:T(8,128)(2,1)} %up.1), custom_call_target="tpu_custom_call" | custom-call | tf_op jit(solution)/shard_map/pallas_call | solution.py:575
  60.3 1.4 %copy.6 = f32[64,128]{1,0:T(8,128)} copy(f32[64,128]{1,0:T(8,128)} %get-tuple-element.4) | data formatting | bytes 65536
  61.6 1.3 %copy.7 = f32[1,1024]{1,0:T(1,128)} copy(f32[1,1024]{1,0:T(1,128)} %get-tuple-element.5) | data formatting | bytes 8192

commit v4 on v3

--- a/solution.py
+++ b/solution.py
@@ -15,7 +15,7 @@
 KA = 6
 KB = UNITS - KA
 PAIRS = UNITS // 2
-A2, A3, AT, BT, BE, AP, BP = 1, 5, 9, 5, 7, 14, 11
+A2, A3, AT, BT, BE, AP, BP = 1, 4, 10, 3, 6, 14, 11
 POWER = 9
 TOP = 2.0**13.8
 MESH = pl.DeviceIdType.MESH
@@ -298,8 +298,9 @@
             src_ref=tokens.at[oc, :, cols], dst_ref=other.at[:, cols], send_sem=other_send,
             recv_sem=other_recv.at[at], device_id=sibling, device_id_type=MESH)
 
-    def each_block(run):
-        for part, (size, _) in enumerate(parts):
+    def each_block(run, which):
+        for part in which:
+            size = parts[part][0]
             def one(i, carry):
                 run(block_at(part, i)[2], starts[part] + i)
                 return carry
@@ -321,8 +322,13 @@
     for to in peers + over_y:
         pl.semaphore_signal(barrier, inc=1, device_id=to, device_id_type=MESH)
     wown_copy.start()
-    each_block(lambda cols, at: own_copy(cols, at).start())
+    pl.semaphore_wait(barrier, len(peers) + len(over_y))
+    wother_copy.start()
+    for which in ((0, 1), (2, 3, 4)):
+        each_block(lambda cols, at: other_copy(cols, at).start(), which)
+        each_block(lambda cols, at: own_copy(cols, at).start(), which)
     up_own.start()
+    up_other.start()
 
     row = lax.broadcasted_iota(jnp.int32, (WINDOW, WINDOW), 0)
     col = lax.broadcasted_iota(jnp.int32, (WINDOW, WINDOW), 1)
@@ -337,10 +343,6 @@
     for ref in (base_z, base_x):
         ref[...] = jnp.full(ref.shape, 1e-33, F32)
 
-    pl.semaphore_wait(barrier, len(peers) + len(over_y))
-    wother_copy.start()
-    each_block(lambda cols, at: other_copy(cols, at).start())
-    up_other.start()
     wother_copy.wait_recv()
     wt[:, depth:] = window(wother)
 
@@ -491,11 +493,11 @@
         bz.near_bounds()
 
     multiply(0)
+    bx.bounds(0)
+    run(b_send(0), 0, KB)
     multiply(1)
     az.bounds(0)
     run(a_send(0), 0, KA)
-    bx.bounds(0)
-    run(b_send(0), 0, KB)
     multiply(2)
     az.bounds(1)
     run(a_send(1), 0, KA)
@@ -517,13 +519,15 @@
         at_tick(at, BP, KB - 1, every_other(b_pair), lambda: bz.all_bounds().wait_recv())
         at_tick(at, AP + 1, half_a, join)
         at_tick(at, BP + 1, KB - 1, every_other(lambda j: join(half_a + j)))
+        at_tick(at, AP + 4, half_a, pass_on)
+        at_tick(at, BP + 5, KB - 1, every_other(lambda j: pass_on(half_a + j)))
         return carry
 
     lax.fori_loop(0, BP + KB, tick, 0)
-    run(pass_on, 0, PAIRS)
-
-    for u in range(UNITS):
-        gram[4 * u:4 * u + 4, :] = gacc[u // 2, 4 * (u % 2):4 * (u % 2) + 4, :]
+    run(pass_on, PAIRS - 2, PAIRS)
+
+    for j in range(PAIRS):
+        gram[8 * j:8 * j + 8, :] = gacc[j]
     all_rows = pltpu.make_async_remote_copy(src_ref=recv2.at[pl.ds(0, CHIPS - 1)], dst_ref=recv2.at[pl.ds(0, CHIPS - 1)],
                                             send_sem=send2, recv_sem=sem2, device_id=sibling, device_id_type=MESH)
     all_rows.wait_send()
@@ -537,9 +541,13 @@
     pltpu.make_async_remote_copy(src_ref=tokens.at[oc], dst_ref=other, send_sem=other_send, recv_sem=other_send,
                                  device_id=sibling, device_id_type=MESH).wait_send()
     all_rows.wait_recv()
-    total = jnp.sum(recv2[...], axis=0)
+    num[...] = jnp.sum(recv2[...], axis=0)
+
+
+def write(gram, num, gram_out, num_out):
+    gram_out[...] = gram[...]
     for i in range(8):
-        num[0:1, 128 * i:128 * (i + 1)] = total[i:i + 1, :]
+        num_out[0:1, 128 * i:128 * (i + 1)] = num[i:i + 1, :]
 
 
 def body(tokens, up_panel):
@@ -576,7 +584,7 @@
         functools.partial(kernel, scale),
         out_shape=(
             jax.ShapeDtypeStruct((WINDOW // NY, block), F32),
-            jax.ShapeDtypeStruct((1, panel), F32),
+            jax.ShapeDtypeStruct((8, panel // 8), F32),
         ),
         in_specs=[pl.BlockSpec(memory_space=pl.ANY)] * 2,
         out_specs=(pl.BlockSpec(memory_space=pltpu.VMEM),) * 2,
@@ -585,7 +593,13 @@
             collective_id=0, has_side_effects=True, vmem_limit_bytes=60 * 2**20
         ),
     )(tokens, up_panel)
-    return gram, num
+    return pl.pallas_call(
+        write,
+        out_shape=(
+            jax.ShapeDtypeStruct((WINDOW // NY, block), F32),
+            jax.ShapeDtypeStruct((1, panel), F32),
+        ),
+    )(gram, num)
 
 
 def solution(mesh):

time: 63.1 us -> 61.6 us (0.976); the launches traced: 62.9 us -> 60.7 us
  local copies, waits for them, and re-layouts: 2.65 us -> 0 us
    unnamed x2 -> x0, local copies, waits for them, and re-layouts: 2.65 us -> none
    pallas_call x0 -> x1, Pallas kernels: none -> 1.38 us  [body(): pl.pallas_call(write, out_shape=(jax.ShapeDtypeStruct((WINDOW // NY, bloc...]
    pallas_call x1, Pallas kernels: 59.6 us -> 58.6 us  [body(): pl.pallas_call(functools.partial(kernel, scale), out_shape=(jax.ShapeDtyp...]
where the time goes in v4:
time: 61.6 us; the launch traced here: 60.7 us
  Pallas kernels  60 us (97%)
  between operations  0.64 us (1%)
    pallas_call x1, Pallas kernels, body(): pl.pallas_call(functools.partial(kernel, scale), out_shape=(jax.ShapeDtyp...  58.6 us
    pallas_call x1, Pallas kernels, body(): pl.pallas_call(write, out_shape=(jax.ShapeDtypeStruct((WINDOW // NY, bloc...  1.38 us

profile of v4, /device:TPU:1, one launch (start us, length us, event | category | flops | bytes accessed | tf_op | source)
XLA Modules:
  0.0 60.7 jit_solution(7139344304642459199)
XLA Ops:
  0.6 58.6 %shard_map.41 = (f32[64,128]{1,0:T(8,128)}, f32[8,128]{1,0:T(8,128)}) custom-call(bf16[2,256,8192]{2,1,0:T(8,128)(2,1)} %tokens.1, bf16[2,128,1024]{2,1,0:T(8,128)(2,1)} %up.1), custom_call_target="tpu_custom_call" | custom-call | tf_op jit(solution)/shard_map/pallas_call | solution.py:583
  59.3 1.4 %shard_map.42 = (f32[64,128]{1,0:T(8,128)}, f32[1,1024]{1,0:T(1,128)}) custom-call(f32[64,128]{1,0:T(8,128)} %get-tuple-element.4.gram, f32[8,128]{1,0:T(8,128)} %get-tuple-element.5.num), custom_call_target="tpu_custom_call" | custom-call | tf_op jit(solution)/shard_map/pallas_call | solution.py:596

commit v5 on v4

--- a/solution.py
+++ b/solution.py
@@ -155,7 +155,7 @@
         enc = TOP / self.bound[...]
         for h in (0, 1):
             self.out[k, :, h] = encode(self.mid[k, h], enc)
-        for o in range(1, self.n):
+        for o in sorted(range(1, self.n), key=lambda o: abs(o - self.n // 2)):
             at, to = self.far(o)
             pltpu.make_async_remote_copy(src_ref=self.out.at[k, at], dst_ref=self.came.at[k, o - 1],
                                          send_sem=self.send_sem.at[k], recv_sem=self.recv_sem.at[k],
@@ -188,7 +188,7 @@
         super().__init__(n, units, me, device, mid, refs[:8])
         self.half = n // 2
         self.pre, self.got, self.near, self.total, self.pre_send, self.pre_recv, self.near_send, self.near_recv = refs[8:]
-        self.others = [o for o in range(1, n) if o != self.half]
+        self.others = sorted((o for o in range(1, n) if o != self.half), key=lambda o: abs(o - self.half))
 
     @staticmethod
     def scratch(n, units):
@@ -394,10 +394,11 @@
 
     def join(j):
         core_copy(j).wait_recv()
-        for p in range(NY):
+        for o in (2, 1, 3, 0):
+            p = lax.rem(y + o, NY)
             msg1[j, c, p] = msg1[j, c, p] + joined[j, p]
-        for o in range(1, NY):
-            p = lax.rem(y + o, NY)
+            if o == 0:
+                break
             pltpu.make_async_remote_copy(src_ref=msg1.at[j, c, p], dst_ref=recv1.at[j, o - 1], send_sem=send1.at[j],
                                          recv_sem=sem1.at[j], device_id=(p, t), device_id_type=MESH).start()
 

time: 61.6 us -> 61.4 us (level)
  no operation moved by 1% of the time
where the time goes in v5:
time: 61.4 us; the launch traced here: 60.5 us
  Pallas kernels  59.9 us (98%)
  between operations  0.64 us (1%)
    pallas_call x1, Pallas kernels, body(): pl.pallas_call(functools.partial(kernel, scale), out_shape=(jax.ShapeDtyp...  58.5 us
    pallas_call x1, Pallas kernels, body(): pl.pallas_call(write, out_shape=(jax.ShapeDtypeStruct((WINDOW // NY, bloc...  1.38 us

profile of v5, /device:TPU:1, one launch (start us, length us, event | category | flops | bytes accessed | tf_op | source)
XLA Modules:
  0.0 60.5 jit_solution(14036849434841574265)
XLA Ops:
  0.6 58.5 %shard_map.41 = (f32[64,128]{1,0:T(8,128)}, f32[8,128]{1,0:T(8,128)}) custom-call(bf16[2,256,8192]{2,1,0:T(8,128)(2,1)} %tokens.1, bf16[2,128,1024]{2,1,0:T(8,128)(2,1)} %up.1), custom_call_target="tpu_custom_call" | custom-call | tf_op jit(solution)/shard_map/pallas_call | solution.py:584
  59.2 1.4 %shard_map.42 = (f32[64,128]{1,0:T(8,128)}, f32[1,1024]{1,0:T(1,128)}) custom-call(f32[64,128]{1,0:T(8,128)} %get-tuple-element.4.gram, f32[8,128]{1,0:T(8,128)} %get-tuple-element.5.num), custom_call_target="tpu_custom_call" | custom-call | tf_op jit(solution)/shard_map/pallas_call | solution.py:597
